TPU v7x, 32 devices: a whole 2x2x4 slice. The times are simulated.
32 devices in a mesh: row: 8 (over z, x), col: 4 (over y, core).
Axes of the slice: x: 2, y: 2, z: 4, core: 2. Of those that a mesh axis runs over, the one named last changes fastest.
Arguments:
- matrix: float32 [2048, 2048], P('row', 'col'), as said below
Outputs:
- factored: float32 [2048, 2048], P('row', 'col')
Inputs may be any that keep to these rules, and one draw needn't show every extreme that they name: `matrix`: each diagonal entry lies between 3 and 6 times the square root of 256; every other entry has magnitude 6 or less.
All inputs are finite; a program needn't handle non-finite values.
Results may differ from a plain program's by a relative error of at most 0.00085.
Values may be sent and summed in bfloat16 or wider, within the bound.
No kernel may reach another device: no remote copies, remote signals or barrier semaphores. Data moves between devices by JAX's collectives and lax.ppermute only.
A program may use at most 64 MiB of HBM per device.

v0:
```python
import jax
import jax.numpy as jnp
from jax import lax
from jax.sharding import PartitionSpec as P

NB = 256
HIGHEST = lax.Precision.HIGHEST
APART = 2


def strides(size):
    out, stride = [], size // 2
    while stride:
        out.append(stride)
        stride //= 2
    return out


def multipliers(square, columns):
    identity = jnp.eye(NB, dtype=jnp.float32)
    diagonal = square * identity
    across = 1.0 / jnp.sum(diagonal, axis=0, keepdims=True)
    down = 1.0 / jnp.sum(diagonal, axis=1, keepdims=True)
    approx = down * (2.0 * identity - square * across)
    rest = 2.0 * identity - jnp.dot(square, approx, precision=HIGHEST)
    return jnp.dot(jnp.dot(columns, approx, precision=HIGHEST), rest, precision=HIGHEST)


def shards(matrix):
    rows_dev, cols_dev = matrix.shape
    assert rows_dev == NB
    n_row, n_col = lax.axis_size("row"), lax.axis_size("col")
    row_here, col_here = lax.axis_index("row"), lax.axis_index("col")

    def send(value, pairs):
        flat = [(r0 * n_col + c0, r1 * n_col + c1) for (r0, c0), (r1, c1) in pairs]
        return lax.ppermute(value, ("row", "col"), flat)

    upper = matrix.astype(jnp.bfloat16)
    pivot_columns, column_upper = lax.optimization_barrier((matrix[:, :NB], upper[:, NB:]))

    down = strides(n_row)
    orders = [down, [down[-1]] + down[:-1]]
    held = [[0], [0]]

    def upper_step(value, step):
        pairs = []
        takes = []
        for kind in range(2):
            stride = orders[kind][step]
            missing = sum(orders[kind][step + 1 :])
            takes.append((row_here & (stride | missing)) == stride)
            pairs += [
                ((h, c), (h + stride, c)) for h in held[kind] for c in range(1, n_col) if c % 2 == kind
            ]
            held[kind] = held[kind] + [h + stride for h in held[kind]]
        got = send(value, pairs)
        return jnp.where(jnp.where(col_here % 2 == 0, takes[0], takes[1]), got, value)

    workers = [r for r in range(n_row) if r & APART == 0]
    targets = workers[1:]
    square, partner = pivot_columns, pivot_columns
    near_upper = column_upper
    upper = upper_step(upper, 0)
    for index, target in enumerate(targets):
        pairs = [((0, 0), (target, 0))]
        if index == 0:
            served = [r for r in workers if r != target]
        elif index == 1:
            served = targets[:1]
        else:
            served = []
        pairs += [((r + APART, 0), (r, 0)) for r in served]
        got = send(pivot_columns, pairs)
        square = jnp.where(row_here == target, got, square)
        if index == 0:
            partner = jnp.where(row_here == target, partner, got)
        elif index == 1:
            partner = jnp.where(row_here == targets[0], got, partner)
    for target in targets:
        got = send(column_upper, [((0, 0), (target, 0))])
        near_upper = jnp.where(row_here == target, got, near_upper)
    upper = upper_step(upper, 1)

    def compute(square, partner):
        both = multipliers(square, jnp.concatenate([pivot_columns, partner], axis=0))
        both = both.astype(jnp.bfloat16)
        return both[:NB], both[NB:]

    def none(square, partner):
        zero = jnp.zeros((NB, NB), jnp.bfloat16)
        return zero, zero

    working = (row_here & APART == 0) & (col_here == 0)
    lower, lower_far = lax.cond(working, compute, none, square, partner)
    received = lower
    for c in range(2, n_col, 2):
        got = send(lower_far, [((r, 0), (r + APART, c)) for r in workers])
        received = jnp.where((row_here & APART != 0) & (col_here == c), got, received)
    both = jnp.concatenate([lower_far, near_upper], axis=1)
    got = send(both, [((r, 0), (r + APART, 0)) for r in workers])
    received = jnp.where((row_here & APART != 0) & (col_here == 0), got[:, :NB], received)
    near_upper = jnp.where(row_here & APART == 0, near_upper, got[:, NB:])
    for c in range(2, n_col, 2):
        got = send(lower, [((r, 0), (r, c)) for r in targets])
        received = jnp.where((row_here & APART == 0) & (col_here == c), got, received)
    for step in range(2, len(down)):
        upper = upper_step(upper, step)
    got = send(
        received, [((r, c), (r, c + 1)) for r in range(1, n_row) for c in range(0, n_col, 2)]
    )
    received = jnp.where(col_here % 2 == 0, received, got)
    received = jnp.where(row_here == 0, jnp.zeros_like(received), received)

    column_upper = jnp.concatenate([jnp.zeros((NB, NB), jnp.bfloat16), near_upper], axis=1)
    upper = jnp.where(col_here == 0, column_upper, upper)
    return matrix - jnp.dot(received, upper, preferred_element_type=jnp.float32)


def solution(mesh):
    return jax.shard_map(
        shards,
        mesh=mesh,
        in_specs=(P("row", "col"),),
        out_specs=P("row", "col"),
        check_vma=False,
    )
```

profile of v0, /device:TPU:29, one launch (start us, length us, event | category | flops | bytes accessed | tf_op | source)
XLA Modules:
  0.0 35.1 jit_solution(14526745344516298721)
XLA Ops:
  0.0 0.0 copy-start
  0.0 1.1 %convert_element_type.12 = bf16[256,512]{1,0:T(8,128)(2,1)S(1)} convert(f32[256,512]{1,0:T(8,128)} %param.3) | non-fusion elementwise | flops 131072 | bytes 786432 | tf_op jit(solution)/shard_map/convert_element_type | solution.py:39
  1.2 0.7 %collective-permute-start.10 = (bf16[256,512]{1,0:T(8,128)(2,1)S(1)}, bf16[256,512]{1,0:T(8,128)(2,1)S(1)}, u32[]{:S(2)}, u32[]{:S(2)}) collective-permute-start(bf16[256,512]{1,0:T(8,128)(2,1)S(1)} %convert_element_type.12), channel_id=1, source_target_pairs={{2,18},{1,5},{3,7}} | collective-permute-start | bytes 786440 | tf_op jit(solution)/shard_map/ppermute | solution.py:37
  1.9 0.0 copy-done
  1.9 0.7 %collective-permute-start.6 = (bf16[256,256]{1,0:T(8,128)(2,1)S(1)}, bf16[256,256]{1,0:T(8,128)(2,1)S(1)}, u32[]{:S(2)}, u32[]{:S(2)}) collective-permute-start(bf16[256,256]{1,0:T(8,128)(2,1)S(1)} %slice.26), channel_id=1, source_target_pairs={{0,4}} | collective-permute-start | bytes 393224 | tf_op jit(solution)/shard_map/ppermute | solution.py:37
  2.6 0.7 %collective-permute-start.5 = (bf16[256,256]{1,0:T(8,128)(2,1)S(1)}, bf16[256,256]{1,0:T(8,128)(2,1)S(1)}, u32[]{:S(2)}, u32[]{:S(2)}) collective-permute-start(bf16[256,256]{1,0:T(8,128)(2,1)S(1)} %slice.26), channel_id=1, source_target_pairs={{0,16}} | collective-permute-start | bytes 393224 | tf_op jit(solution)/shard_map/ppermute | solution.py:37
  3.2 0.7 %collective-permute-start.4 = (bf16[256,256]{1,0:T(8,128)(2,1)S(1)}, bf16[256,256]{1,0:T(8,128)(2,1)S(1)}, u32[]{:S(2)}, u32[]{:S(2)}) collective-permute-start(bf16[256,256]{1,0:T(8,128)(2,1)S(1)} %slice.26), channel_id=1, source_target_pairs={{0,20}} | collective-permute-start | bytes 393224 | tf_op jit(solution)/shard_map/ppermute | solution.py:37
  3.9 0.7 %collective-permute-start.2 = (f32[256,256]{1,0:T(8,128)S(1)}, f32[256,256]{1,0:T(8,128)S(1)}, u32[]{:S(2)}, u32[]{:S(2)}) collective-permute-start(f32[256,256]{1,0:T(8,128)S(1)} %slice.20), channel_id=1, source_target_pairs={{0,20}} | collective-permute-start | bytes 786440 | tf_op jit(solution)/shard_map/ppermute | solution.py:37
  4.6 0.0 collective-permute-done.6
  4.7 0.7 %collective-permute-start.1 = (f32[256,256]{1,0:T(8,128)S(1)}, f32[256,256]{1,0:T(8,128)S(1)}, u32[]{:S(2)}, u32[]{:S(2)}) collective-permute-start(f32[256,256]{1,0:T(8,128)S(1)} %slice.20), channel_id=1, source_target_pairs={{0,16},{12,4}} | collective-permute-start | bytes 786440 | tf_op jit(solution)/shard_map/ppermute | solution.py:37
  5.3 0.0 collective-permute-done.10
  5.4 0.7 %collective-permute-start = (f32[256,256]{1,0:T(8,128)S(1)}, f32[256,256]{1,0:T(8,128)S(1)}, u32[]{:S(2)}, u32[]{:S(2)}) collective-permute-start(f32[256,256]{1,0:T(8,128)S(1)} %slice.20), channel_id=1, source_target_pairs={{0,4},{8,0},{24,16},{28,20}} | collective-permute-start | bytes 786440 | tf_op jit(solution)/shard_map/ppermute | solution.py:37
  6.1 0.0 collective-permute-done.5
  6.1 0.7 %collective-permute-start.11 = (bf16[256,512]{1,0:T(8,128)(2,1)S(1)}, bf16[256,512]{1,0:T(8,128)(2,1)S(1)}, u32[]{:S(2)}, u32[]{:S(2)}) collective-permute-start(bf16[256,512]{1,0:T(8,128)(2,1)S(1)} %broadcast_select_fusion), channel_id=1, source_target_pairs={{2,10},{18,26},{1,17},{3,19},{5,21},{7,23}} | collective-permute-start | bytes 786440 | tf_op jit(solution)/shard_map/ppermute | solution.py:37
  6.8 0.0 collective-permute-done.4
  6.8 0.0 collective-permute-done.2
  6.8 0.0 collective-permute-done.1
  6.9 0.0 collective-permute-done
  6.9 0.1 conditional.1
  7.0 0.7 %collective-permute-start.7 = (bf16[256,512]{1,0:T(8,128)(2,1)S(1)}, bf16[256,512]{1,0:T(8,128)(2,1)S(1)}, u32[]{:S(2)}, u32[]{:S(2)}) collective-permute-start(bf16[256,512]{1,0:T(8,128)(2,1)S(1)} %pad_maximum_fusion), channel_id=1, source_target_pairs={{0,8},{4,12},{16,24},{20,28}} | collective-permute-start | bytes 786440 | tf_op jit(solution)/shard_map/ppermute | solution.py:37
  7.7 0.7 %collective-permute-start.8 = (bf16[256,256]{1,0:T(8,128)(2,1)S(1)}, bf16[256,256]{1,0:T(8,128)(2,1)S(1)}, u32[]{:S(2)}, u32[]{:S(2)}) collective-permute-start(bf16[256,256]{1,0:T(8,128)(2,1)S(1)} %get-tuple-element.66), channel_id=1, source_target_pairs={{0,10},{4,14},{16,26},{20,30}} | collective-permute-start | bytes 393224 | tf_op jit(solution)/shard_map/ppermute | solution.py:37
  8.4 0.7 %collective-permute-start.3 = (bf16[256,256]{1,0:T(8,128)(2,1)S(1)}, bf16[256,256]{1,0:T(8,128)(2,1)S(1)}, u32[]{:S(2)}, u32[]{:S(2)}) collective-permute-start(bf16[256,256]{1,0:T(8,128)(2,1)S(1)} %get-tuple-element.65), channel_id=1, source_target_pairs={{4,6},{16,18},{20,22}} | collective-permute-start | bytes 393224 | tf_op jit(solution)/shard_map/ppermute | solution.py:37
  9.1 0.0 collective-permute-done.11
  9.1 1.3 %collective-permute-start.12 = (bf16[256,512]{1,0:T(8,128)(2,1)S(1)}, bf16[256,512]{1,0:T(8,128)(2,1)S(1)}, u32[]{:S(2)}, u32[]{:S(2)}) collective-permute-start(bf16[256,512]{1,0:T(8,128)(2,1)S(1)} %broadcast_select_fusion.1), channel_id=1, source_target_pairs={{2,6},{18,22},{10,14},{26,30},{1,9},{3,11},{5,13},{7,15},{17,25},{... | collective-permute-start | bytes 786440 | tf_op jit(solution)/shard_map/ppermute | solution.py:37
  10.4 0.0 collective-permute-done.3
  10.4 0.0 collective-permute-done.8
  10.4 0.0 collective-permute-done.7
  10.5 0.1 fusion.28
  10.5 1.3 %collective-permute-start.9 = (bf16[256,256]{1,0:T(8,128)(2,1)S(1)}, bf16[256,256]{1,0:T(8,128)(2,1)S(1)}, u32[]{:S(2)}, u32[]{:S(2)}) collective-permute-start(bf16[256,256]{1,0:T(8,128)(2,1)S(1)} %get-tuple-element.76), channel_id=1, source_target_pairs={{4,5},{6,7},{8,9},{10,11},{12,13},{14,15},{16,17},{18,19},{20,21},... | collective-permute-start | bytes 393224 | tf_op jit(solution)/shard_map/ppermute | solution.py:37
  11.8 22.2 %collective-permute-done.9 = bf16[256,256]{1,0:T(8,128)(2,1)S(1)} collective-permute-done((bf16[256,256]{1,0:T(8,128)(2,1)S(1)}, bf16[256,256]{1,0:T(8,128)(2,1)S(1)}, u32[]{:S(2)}, u32[]{:S(2)}) %collective-permute-start.9) | collective-permute-done | bytes 131104 | tf_op jit(solution)/shard_map/ppermute | solution.py:37
  34.1 0.0 collective-permute-done.12
  34.1 1.1 %convolution_subtract_fusion.1 = f32[256,512]{1,0:T(8,128)} fusion(f32[256,512]{1,0:T(8,128)S(1)} %copy-done, bf16[256,512]{1,0:T(8,128)(2,1)S(1)} %collective-permute-done.12, bf16[256,512]{1,0:T(8,128)(2,1)S(1)} %broadcast_select_fusion.1, bf16[256,256]{1,0:T(8,128)(2,1)S(1)} %get-tuple-element.77, pred[]{:T(512)S(6)} %select_n.161, pred[]{:T(512)S(6)} %eq.72, ...), kind=kOutput, calls=%fused_computation.29 | convolution fusion | flops 67633152 | bytes 1966084 | tf_op jit(solution)/shard_map/dot_general | solution.py:117
  (10 shorter events, 0.2 us)
Async XLA Ops:
  0.0 1.9 %copy-start = (f32[256,512]{1,0:T(8,128)S(1)}, f32[256,512]{1,0:T(8,128)}, u32[]{:S(2)}) copy-start(f32[256,512]{1,0:T(8,128)} %param.3) | copy-start | bytes 1572868
  1.2 4.2 %collective-permute-start.10 = (bf16[256,512]{1,0:T(8,128)(2,1)S(1)}, bf16[256,512]{1,0:T(8,128)(2,1)S(1)}, u32[]{:S(2)}, u32[]{:S(2)}) collective-permute-start(bf16[256,512]{1,0:T(8,128)(2,1)S(1)} %convert_element_type.12), channel_id=1, source_target_pairs={{2,18},{1,5},{3,7}} | collective-permute-start | bytes 786440 | tf_op jit(solution)/shard_map/ppermute | solution.py:37
  1.9 2.8 %collective-permute-start.6 = (bf16[256,256]{1,0:T(8,128)(2,1)S(1)}, bf16[256,256]{1,0:T(8,128)(2,1)S(1)}, u32[]{:S(2)}, u32[]{:S(2)}) collective-permute-start(bf16[256,256]{1,0:T(8,128)(2,1)S(1)} %slice.26), channel_id=1, source_target_pairs={{0,4}} | collective-permute-start | bytes 393224 | tf_op jit(solution)/shard_map/ppermute | solution.py:37
  2.6 3.5 %collective-permute-start.5 = (bf16[256,256]{1,0:T(8,128)(2,1)S(1)}, bf16[256,256]{1,0:T(8,128)(2,1)S(1)}, u32[]{:S(2)}, u32[]{:S(2)}) collective-permute-start(bf16[256,256]{1,0:T(8,128)(2,1)S(1)} %slice.26), channel_id=1, source_target_pairs={{0,16}} | collective-permute-start | bytes 393224 | tf_op jit(solution)/shard_map/ppermute | solution.py:37
  3.2 3.5 %collective-permute-start.4 = (bf16[256,256]{1,0:T(8,128)(2,1)S(1)}, bf16[256,256]{1,0:T(8,128)(2,1)S(1)}, u32[]{:S(2)}, u32[]{:S(2)}) collective-permute-start(bf16[256,256]{1,0:T(8,128)(2,1)S(1)} %slice.26), channel_id=1, source_target_pairs={{0,20}} | collective-permute-start | bytes 393224 | tf_op jit(solution)/shard_map/ppermute | solution.py:37
  3.9 2.9 %collective-permute-start.2 = (f32[256,256]{1,0:T(8,128)S(1)}, f32[256,256]{1,0:T(8,128)S(1)}, u32[]{:S(2)}, u32[]{:S(2)}) collective-permute-start(f32[256,256]{1,0:T(8,128)S(1)} %slice.20), channel_id=1, source_target_pairs={{0,20}} | collective-permute-start | bytes 786440 | tf_op jit(solution)/shard_map/ppermute | solution.py:37
  4.7 2.2 %collective-permute-start.1 = (f32[256,256]{1,0:T(8,128)S(1)}, f32[256,256]{1,0:T(8,128)S(1)}, u32[]{:S(2)}, u32[]{:S(2)}) collective-permute-start(f32[256,256]{1,0:T(8,128)S(1)} %slice.20), channel_id=1, source_target_pairs={{0,16},{12,4}} | collective-permute-start | bytes 786440 | tf_op jit(solution)/shard_map/ppermute | solution.py:37
  5.4 1.5 %collective-permute-start = (f32[256,256]{1,0:T(8,128)S(1)}, f32[256,256]{1,0:T(8,128)S(1)}, u32[]{:S(2)}, u32[]{:S(2)}) collective-permute-start(f32[256,256]{1,0:T(8,128)S(1)} %slice.20), channel_id=1, source_target_pairs={{0,4},{8,0},{24,16},{28,20}} | collective-permute-start | bytes 786440 | tf_op jit(solution)/shard_map/ppermute | solution.py:37
  6.1 3.0 %collective-permute-start.11 = (bf16[256,512]{1,0:T(8,128)(2,1)S(1)}, bf16[256,512]{1,0:T(8,128)(2,1)S(1)}, u32[]{:S(2)}, u32[]{:S(2)}) collective-permute-start(bf16[256,512]{1,0:T(8,128)(2,1)S(1)} %broadcast_select_fusion), channel_id=1, source_target_pairs={{2,10},{18,26},{1,17},{3,19},{5,21},{7,23}} | collective-permute-start | bytes 786440 | tf_op jit(solution)/shard_map/ppermute | solution.py:37
  7.0 3.4 %collective-permute-start.7 = (bf16[256,512]{1,0:T(8,128)(2,1)S(1)}, bf16[256,512]{1,0:T(8,128)(2,1)S(1)}, u32[]{:S(2)}, u32[]{:S(2)}) collective-permute-start(bf16[256,512]{1,0:T(8,128)(2,1)S(1)} %pad_maximum_fusion), channel_id=1, source_target_pairs={{0,8},{4,12},{16,24},{20,28}} | collective-permute-start | bytes 786440 | tf_op jit(solution)/shard_map/ppermute | solution.py:37
  7.7 2.7 %collective-permute-start.8 = (bf16[256,256]{1,0:T(8,128)(2,1)S(1)}, bf16[256,256]{1,0:T(8,128)(2,1)S(1)}, u32[]{:S(2)}, u32[]{:S(2)}) collective-permute-start(bf16[256,256]{1,0:T(8,128)(2,1)S(1)} %get-tuple-element.66), channel_id=1, source_target_pairs={{0,10},{4,14},{16,26},{20,30}} | collective-permute-start | bytes 393224 | tf_op jit(solution)/shard_map/ppermute | solution.py:37
  8.4 2.0 %collective-permute-start.3 = (bf16[256,256]{1,0:T(8,128)(2,1)S(1)}, bf16[256,256]{1,0:T(8,128)(2,1)S(1)}, u32[]{:S(2)}, u32[]{:S(2)}) collective-permute-start(bf16[256,256]{1,0:T(8,128)(2,1)S(1)} %get-tuple-element.65), channel_id=1, source_target_pairs={{4,6},{16,18},{20,22}} | collective-permute-start | bytes 393224 | tf_op jit(solution)/shard_map/ppermute | solution.py:37
  9.1 24.9 %collective-permute-start.12 = (bf16[256,512]{1,0:T(8,128)(2,1)S(1)}, bf16[256,512]{1,0:T(8,128)(2,1)S(1)}, u32[]{:S(2)}, u32[]{:S(2)}) collective-permute-start(bf16[256,512]{1,0:T(8,128)(2,1)S(1)} %broadcast_select_fusion.1), channel_id=1, source_target_pairs={{2,6},{18,22},{10,14},{26,30},{1,9},{3,11},{5,13},{7,15},{17,25},{... | collective-permute-start | bytes 786440 | tf_op jit(solution)/shard_map/ppermute | solution.py:37
  10.5 23.5 %collective-permute-start.9 = (bf16[256,256]{1,0:T(8,128)(2,1)S(1)}, bf16[256,256]{1,0:T(8,128)(2,1)S(1)}, u32[]{:S(2)}, u32[]{:S(2)}) collective-permute-start(bf16[256,256]{1,0:T(8,128)(2,1)S(1)} %get-tuple-element.76), channel_id=1, source_target_pairs={{4,5},{6,7},{8,9},{10,11},{12,13},{14,15},{16,17},{18,19},{20,21},... | collective-permute-start | bytes 393224 | tf_op jit(solution)/shard_map/ppermute | solution.py:37
where the time goes:
time: 35.5 us; the launch traced here: 35.1 us
  waiting for transfers between devices  22.3 us (63%)
  starting transfers between devices  9.99 us (28%)
  other arithmetic  1.32 us (4%)
  matrix products  1.07 us (3%)
  between operations  0.36 us (1%)
    ppermute x13, waiting for transfers between devices, send(): return lax.ppermute(value, ('row', 'col'), flat)  22.3 us
    ppermute x13, starting transfers between devices, send(): return lax.ppermute(value, ('row', 'col'), flat)  9.99 us
    convert_element_type x1, other arithmetic, shards(): upper = matrix.astype(jnp.bfloat16)  1.15 us
    dot_general x1, matrix products, shards(): return matrix - jnp.dot(received, upper, preferred_element_type=jnp.float32)  1.07 us
  transfers between devices with their start and end apart: 13, of which 1 were waited for; matrix products, arithmetic and copies ran while one was open for 1% of the time, Pallas kernels for 0%

commit v1 on v0

--- a/solution.py
+++ b/solution.py
@@ -37,7 +37,7 @@
         return lax.ppermute(value, ("row", "col"), flat)
 
     upper = matrix.astype(jnp.bfloat16)
-    pivot_columns, column_upper = lax.optimization_barrier((matrix[:, :NB], upper[:, NB:]))
+    pivot_columns, column_upper = matrix[:, :NB], upper[:, NB:]
 
     down = strides(n_row)
     orders = [down, [down[-1]] + down[:-1]]
@@ -61,7 +61,7 @@
     targets = workers[1:]
     square, partner = pivot_columns, pivot_columns
     near_upper = column_upper
-    upper = upper_step(upper, 0)
+    upper, column_upper = lax.optimization_barrier((upper_step(upper, 0), column_upper))
     for index, target in enumerate(targets):
         pairs = [((0, 0), (target, 0))]
         if index == 0:

time: 35.5 us -> 32.8 us (0.924)
  waiting for transfers between devices: 22.3 us -> 19.6 us
    ppermute x13, waiting for transfers between devices: 22.3 us -> 19.6 us  [send(): return lax.ppermute(value, ('row', 'col'), flat)]
  transfers between devices with their start and end apart: 13 -> 13, of which waited for: 1 -> 2; matrix products, arithmetic and copies ran while one was open for 1% -> 1% of each run, Pallas kernels for 0% -> 0%
where the time goes in v1:
time: 32.8 us; the launch traced here: 32.5 us
  waiting for transfers between devices  19.6 us (60%)
  starting transfers between devices  9.99 us (30%)
  other arithmetic  1.32 us (4%)
  matrix products  1.07 us (3%)
  between operations  0.38 us (1%)
    ppermute x13, waiting for transfers between devices, send(): return lax.ppermute(value, ('row', 'col'), flat)  19.6 us
    ppermute x13, starting transfers between devices, send(): return lax.ppermute(value, ('row', 'col'), flat)  9.99 us
    convert_element_type x1, other arithmetic, shards(): upper = matrix.astype(jnp.bfloat16)  1.15 us
    dot_general x1, matrix products, shards(): return matrix - jnp.dot(received, upper, preferred_element_type=jnp.float32)  1.07 us
  transfers between devices with their start and end apart: 13, of which 2 were waited for; matrix products, arithmetic and copies ran while one was open for 1% of the time, Pallas kernels for 0%

profile of v1, /device:TPU:29, one launch (start us, length us, event | category | flops | bytes accessed | tf_op | source)
XLA Modules:
  0.0 32.5 jit_solution(14404098357687238631)
XLA Ops:
  0.0 0.0 copy-start
  0.0 1.1 %convert_element_type.12 = bf16[256,512]{1,0:T(8,128)(2,1)S(1)} convert(f32[256,512]{1,0:T(8,128)} %param.3) | non-fusion elementwise | flops 131072 | bytes 786432 | tf_op jit(solution)/shard_map/convert_element_type | solution.py:39
  1.2 0.7 %collective-permute-start.4 = (bf16[256,512]{1,0:T(8,128)(2,1)S(1)}, bf16[256,512]{1,0:T(8,128)(2,1)S(1)}, u32[]{:S(2)}, u32[]{:S(2)}) collective-permute-start(bf16[256,512]{1,0:T(8,128)(2,1)S(1)} %convert_element_type.12), channel_id=1, source_target_pairs={{2,18},{1,5},{3,7}} | collective-permute-start | bytes 786440 | tf_op jit(solution)/shard_map/ppermute | solution.py:37
  1.8 0.0 copy-done
  1.9 0.7 %collective-permute-start = (f32[256,256]{1,0:T(8,128)S(1)}, f32[256,256]{1,0:T(8,128)S(1)}, u32[]{:S(2)}, u32[]{:S(2)}) collective-permute-start(f32[256,256]{1,0:T(8,128)S(1)} %slice.20), channel_id=1, source_target_pairs={{0,4},{8,0},{24,16},{28,20}} | collective-permute-start | bytes 786440 | tf_op jit(solution)/shard_map/ppermute | solution.py:37
  2.6 0.7 %collective-permute-start.1 = (f32[256,256]{1,0:T(8,128)S(1)}, f32[256,256]{1,0:T(8,128)S(1)}, u32[]{:S(2)}, u32[]{:S(2)}) collective-permute-start(f32[256,256]{1,0:T(8,128)S(1)} %slice.20), channel_id=1, source_target_pairs={{0,16},{12,4}} | collective-permute-start | bytes 786440 | tf_op jit(solution)/shard_map/ppermute | solution.py:37
  3.2 0.7 %collective-permute-start.2 = (f32[256,256]{1,0:T(8,128)S(1)}, f32[256,256]{1,0:T(8,128)S(1)}, u32[]{:S(2)}, u32[]{:S(2)}) collective-permute-start(f32[256,256]{1,0:T(8,128)S(1)} %slice.20), channel_id=1, source_target_pairs={{0,20}} | collective-permute-start | bytes 786440 | tf_op jit(solution)/shard_map/ppermute | solution.py:37
  4.0 0.0 collective-permute-done.4
  4.0 0.7 %collective-permute-start.5 = (bf16[256,256]{1,0:T(8,128)(2,1)S(1)}, bf16[256,256]{1,0:T(8,128)(2,1)S(1)}, u32[]{:S(2)}, u32[]{:S(2)}) collective-permute-start(bf16[256,256]{1,0:T(8,128)(2,1)S(1)} %slice.26), channel_id=1, source_target_pairs={{0,20}} | collective-permute-start | bytes 393224 | tf_op jit(solution)/shard_map/ppermute | solution.py:37
  4.7 0.7 %collective-permute-start.6 = (bf16[256,256]{1,0:T(8,128)(2,1)S(1)}, bf16[256,256]{1,0:T(8,128)(2,1)S(1)}, u32[]{:S(2)}, u32[]{:S(2)}) collective-permute-start(bf16[256,256]{1,0:T(8,128)(2,1)S(1)} %slice.26), channel_id=1, source_target_pairs={{0,16}} | collective-permute-start | bytes 393224 | tf_op jit(solution)/shard_map/ppermute | solution.py:37
  5.4 0.0 collective-permute-done
  5.4 0.7 %collective-permute-start.7 = (bf16[256,256]{1,0:T(8,128)(2,1)S(1)}, bf16[256,256]{1,0:T(8,128)(2,1)S(1)}, u32[]{:S(2)}, u32[]{:S(2)}) collective-permute-start(bf16[256,256]{1,0:T(8,128)(2,1)S(1)} %slice.26), channel_id=1, source_target_pairs={{0,4}} | collective-permute-start | bytes 393224 | tf_op jit(solution)/shard_map/ppermute | solution.py:37
  6.1 0.0 collective-permute-done.1
  6.1 0.7 %collective-permute-start.11 = (bf16[256,512]{1,0:T(8,128)(2,1)S(1)}, bf16[256,512]{1,0:T(8,128)(2,1)S(1)}, u32[]{:S(2)}, u32[]{:S(2)}) collective-permute-start(bf16[256,512]{1,0:T(8,128)(2,1)S(1)} %broadcast_select_fusion.1), channel_id=1, source_target_pairs={{2,10},{18,26},{1,17},{3,19},{5,21},{7,23}} | collective-permute-start | bytes 786440 | tf_op jit(solution)/shard_map/ppermute | solution.py:37
  6.8 0.0 collective-permute-done.2
  6.9 0.1 conditional.1
  6.9 0.0 collective-permute-done.5
  6.9 0.0 collective-permute-done.6
  6.9 0.0 collective-permute-done.7
  7.0 0.7 %collective-permute-start.8 = (bf16[256,512]{1,0:T(8,128)(2,1)S(1)}, bf16[256,512]{1,0:T(8,128)(2,1)S(1)}, u32[]{:S(2)}, u32[]{:S(2)}) collective-permute-start(bf16[256,512]{1,0:T(8,128)(2,1)S(1)} %pad_maximum_fusion), channel_id=1, source_target_pairs={{0,8},{4,12},{16,24},{20,28}} | collective-permute-start | bytes 786440 | tf_op jit(solution)/shard_map/ppermute | solution.py:37
  7.7 0.7 %collective-permute-start.9 = (bf16[256,256]{1,0:T(8,128)(2,1)S(1)}, bf16[256,256]{1,0:T(8,128)(2,1)S(1)}, u32[]{:S(2)}, u32[]{:S(2)}) collective-permute-start(bf16[256,256]{1,0:T(8,128)(2,1)S(1)} %get-tuple-element.65), channel_id=1, source_target_pairs={{0,10},{4,14},{16,26},{20,30}} | collective-permute-start | bytes 393224 | tf_op jit(solution)/shard_map/ppermute | solution.py:37
  8.4 0.7 %collective-permute-start.3 = (bf16[256,256]{1,0:T(8,128)(2,1)S(1)}, bf16[256,256]{1,0:T(8,128)(2,1)S(1)}, u32[]{:S(2)}, u32[]{:S(2)}) collective-permute-start(bf16[256,256]{1,0:T(8,128)(2,1)S(1)} %get-tuple-element.64), channel_id=1, source_target_pairs={{4,6},{16,18},{20,22}} | collective-permute-start | bytes 393224 | tf_op jit(solution)/shard_map/ppermute | solution.py:37
  9.1 0.0 collective-permute-done.11
  9.1 1.3 %collective-permute-start.12 = (bf16[256,512]{1,0:T(8,128)(2,1)S(1)}, bf16[256,512]{1,0:T(8,128)(2,1)S(1)}, u32[]{:S(2)}, u32[]{:S(2)}) collective-permute-start(bf16[256,512]{1,0:T(8,128)(2,1)S(1)} %broadcast_select_fusion), channel_id=1, source_target_pairs={{2,6},{18,22},{10,14},{26,30},{1,9},{3,11},{5,13},{7,15},{17,25},{... | collective-permute-start | bytes 786440 | tf_op jit(solution)/shard_map/ppermute | solution.py:37
  10.4 0.0 collective-permute-done.3
  10.5 0.0 collective-permute-done.9
  10.5 0.0 collective-permute-done.8
  10.5 0.1 fusion.28
  10.5 1.3 %collective-permute-start.10 = (bf16[256,256]{1,0:T(8,128)(2,1)S(1)}, bf16[256,256]{1,0:T(8,128)(2,1)S(1)}, u32[]{:S(2)}, u32[]{:S(2)}) collective-permute-start(bf16[256,256]{1,0:T(8,128)(2,1)S(1)} %get-tuple-element.76), channel_id=1, source_target_pairs={{4,5},{6,7},{8,9},{10,11},{12,13},{14,15},{16,17},{18,19},{20,21},... | collective-permute-start | bytes 393224 | tf_op jit(solution)/shard_map/ppermute | solution.py:37
  11.8 9.5 %collective-permute-done.12 = bf16[256,512]{1,0:T(8,128)(2,1)S(1)} collective-permute-done((bf16[256,512]{1,0:T(8,128)(2,1)S(1)}, bf16[256,512]{1,0:T(8,128)(2,1)S(1)}, u32[]{:S(2)}, u32[]{:S(2)}) %collective-permute-start.12) | collective-permute-done | bytes 262176 | tf_op jit(solution)/shard_map/ppermute | solution.py:37
  21.3 10.1 %collective-permute-done.10 = bf16[256,256]{1,0:T(8,128)(2,1)S(1)} collective-permute-done((bf16[256,256]{1,0:T(8,128)(2,1)S(1)}, bf16[256,256]{1,0:T(8,128)(2,1)S(1)}, u32[]{:S(2)}, u32[]{:S(2)}) %collective-permute-start.10) | collective-permute-done | bytes 131104 | tf_op jit(solution)/shard_map/ppermute | solution.py:37
  31.4 1.1 %convolution_subtract_fusion.1 = f32[256,512]{1,0:T(8,128)} fusion(f32[256,512]{1,0:T(8,128)S(1)} %copy-done, bf16[256,512]{1,0:T(8,128)(2,1)S(1)} %collective-permute-done.12, bf16[256,512]{1,0:T(8,128)(2,1)S(1)} %broadcast_select_fusion, bf16[256,256]{1,0:T(8,128)(2,1)S(1)} %get-tuple-element.77, pred[]{:T(512)S(6)} %select_n.164, pred[]{:T(512)S(6)} %eq.72, ...), kind=kOutput, calls=%fused_computation.29 | convolution fusion | flops 67633152 | bytes 1966084 | tf_op jit(solution)/shard_map/dot_general | solution.py:117
  (10 shorter events, 0.2 us)
Async XLA Ops:
  0.0 1.8 %copy-start = (f32[256,512]{1,0:T(8,128)S(1)}, f32[256,512]{1,0:T(8,128)}, u32[]{:S(2)}) copy-start(f32[256,512]{1,0:T(8,128)} %param.3) | copy-start | bytes 1572868
  1.2 2.8 %collective-permute-start.4 = (bf16[256,512]{1,0:T(8,128)(2,1)S(1)}, bf16[256,512]{1,0:T(8,128)(2,1)S(1)}, u32[]{:S(2)}, u32[]{:S(2)}) collective-permute-start(bf16[256,512]{1,0:T(8,128)(2,1)S(1)} %convert_element_type.12), channel_id=1, source_target_pairs={{2,18},{1,5},{3,7}} | collective-permute-start | bytes 786440 | tf_op jit(solution)/shard_map/ppermute | solution.py:37
  1.9 3.5 %collective-permute-start = (f32[256,256]{1,0:T(8,128)S(1)}, f32[256,256]{1,0:T(8,128)S(1)}, u32[]{:S(2)}, u32[]{:S(2)}) collective-permute-start(f32[256,256]{1,0:T(8,128)S(1)} %slice.20), channel_id=1, source_target_pairs={{0,4},{8,0},{24,16},{28,20}} | collective-permute-start | bytes 786440 | tf_op jit(solution)/shard_map/ppermute | solution.py:37
  2.6 3.5 %collective-permute-start.1 = (f32[256,256]{1,0:T(8,128)S(1)}, f32[256,256]{1,0:T(8,128)S(1)}, u32[]{:S(2)}, u32[]{:S(2)}) collective-permute-start(f32[256,256]{1,0:T(8,128)S(1)} %slice.20), channel_id=1, source_target_pairs={{0,16},{12,4}} | collective-permute-start | bytes 786440 | tf_op jit(solution)/shard_map/ppermute | solution.py:37
  3.2 3.6 %collective-permute-start.2 = (f32[256,256]{1,0:T(8,128)S(1)}, f32[256,256]{1,0:T(8,128)S(1)}, u32[]{:S(2)}, u32[]{:S(2)}) collective-permute-start(f32[256,256]{1,0:T(8,128)S(1)} %slice.20), channel_id=1, source_target_pairs={{0,20}} | collective-permute-start | bytes 786440 | tf_op jit(solution)/shard_map/ppermute | solution.py:37
  4.0 2.9 %collective-permute-start.5 = (bf16[256,256]{1,0:T(8,128)(2,1)S(1)}, bf16[256,256]{1,0:T(8,128)(2,1)S(1)}, u32[]{:S(2)}, u32[]{:S(2)}) collective-permute-start(bf16[256,256]{1,0:T(8,128)(2,1)S(1)} %slice.26), channel_id=1, source_target_pairs={{0,20}} | collective-permute-start | bytes 393224 | tf_op jit(solution)/shard_map/ppermute | solution.py:37
  4.7 2.2 %collective-permute-start.6 = (bf16[256,256]{1,0:T(8,128)(2,1)S(1)}, bf16[256,256]{1,0:T(8,128)(2,1)S(1)}, u32[]{:S(2)}, u32[]{:S(2)}) collective-permute-start(bf16[256,256]{1,0:T(8,128)(2,1)S(1)} %slice.26), channel_id=1, source_target_pairs={{0,16}} | collective-permute-start | bytes 393224 | tf_op jit(solution)/shard_map/ppermute | solution.py:37
  5.4 1.5 %collective-permute-start.7 = (bf16[256,256]{1,0:T(8,128)(2,1)S(1)}, bf16[256,256]{1,0:T(8,128)(2,1)S(1)}, u32[]{:S(2)}, u32[]{:S(2)}) collective-permute-start(bf16[256,256]{1,0:T(8,128)(2,1)S(1)} %slice.26), channel_id=1, source_target_pairs={{0,4}} | collective-permute-start | bytes 393224 | tf_op jit(solution)/shard_map/ppermute | solution.py:37
  6.1 3.0 %collective-permute-start.11 = (bf16[256,512]{1,0:T(8,128)(2,1)S(1)}, bf16[256,512]{1,0:T(8,128)(2,1)S(1)}, u32[]{:S(2)}, u32[]{:S(2)}) collective-permute-start(bf16[256,512]{1,0:T(8,128)(2,1)S(1)} %broadcast_select_fusion.1), channel_id=1, source_target_pairs={{2,10},{18,26},{1,17},{3,19},{5,21},{7,23}} | collective-permute-start | bytes 786440 | tf_op jit(solution)/shard_map/ppermute | solution.py:37
  7.0 3.4 %collective-permute-start.8 = (bf16[256,512]{1,0:T(8,128)(2,1)S(1)}, bf16[256,512]{1,0:T(8,128)(2,1)S(1)}, u32[]{:S(2)}, u32[]{:S(2)}) collective-permute-start(bf16[256,512]{1,0:T(8,128)(2,1)S(1)} %pad_maximum_fusion), channel_id=1, source_target_pairs={{0,8},{4,12},{16,24},{20,28}} | collective-permute-start | bytes 786440 | tf_op jit(solution)/shard_map/ppermute | solution.py:37
  7.7 2.7 %collective-permute-start.9 = (bf16[256,256]{1,0:T(8,128)(2,1)S(1)}, bf16[256,256]{1,0:T(8,128)(2,1)S(1)}, u32[]{:S(2)}, u32[]{:S(2)}) collective-permute-start(bf16[256,256]{1,0:T(8,128)(2,1)S(1)} %get-tuple-element.65), channel_id=1, source_target_pairs={{0,10},{4,14},{16,26},{20,30}} | collective-permute-start | bytes 393224 | tf_op jit(solution)/shard_map/ppermute | solution.py:37
  8.4 2.0 %collective-permute-start.3 = (bf16[256,256]{1,0:T(8,128)(2,1)S(1)}, bf16[256,256]{1,0:T(8,128)(2,1)S(1)}, u32[]{:S(2)}, u32[]{:S(2)}) collective-permute-start(bf16[256,256]{1,0:T(8,128)(2,1)S(1)} %get-tuple-element.64), channel_id=1, source_target_pairs={{4,6},{16,18},{20,22}} | collective-permute-start | bytes 393224 | tf_op jit(solution)/shard_map/ppermute | solution.py:37
  9.1 12.2 %collective-permute-start.12 = (bf16[256,512]{1,0:T(8,128)(2,1)S(1)}, bf16[256,512]{1,0:T(8,128)(2,1)S(1)}, u32[]{:S(2)}, u32[]{:S(2)}) collective-permute-start(bf16[256,512]{1,0:T(8,128)(2,1)S(1)} %broadcast_select_fusion), channel_id=1, source_target_pairs={{2,6},{18,22},{10,14},{26,30},{1,9},{3,11},{5,13},{7,15},{17,25},{... | collective-permute-start | bytes 786440 | tf_op jit(solution)/shard_map/ppermute | solution.py:37
  10.5 20.9 %collective-permute-start.10 = (bf16[256,256]{1,0:T(8,128)(2,1)S(1)}, bf16[256,256]{1,0:T(8,128)(2,1)S(1)}, u32[]{:S(2)}, u32[]{:S(2)}) collective-permute-start(bf16[256,256]{1,0:T(8,128)(2,1)S(1)} %get-tuple-element.76), channel_id=1, source_target_pairs={{4,5},{6,7},{8,9},{10,11},{12,13},{14,15},{16,17},{18,19},{20,21},... | collective-permute-start | bytes 393224 | tf_op jit(solution)/shard_map/ppermute | solution.py:37
